TPU v7x, 512 devices: a whole 4x8x8 slice. The times are simulated.
512 devices in a mesh: inst: 16 (over z_lo, x, core), blk: 32 (over y, z_hi).
Axes of the slice: x: 4, y: 8, z: 8 (z_hi: 4, z_lo: 2; z = z_hi * 2 + z_lo), core: 2. Of those that a mesh axis runs over, the one named last changes fastest.
Arguments:
- state: float32 [16, 5, 16, 256, 256], P('inst', None, None, 'blk'), may hold values from -0.53 to 3.9, as said below
- multiples: int32 [7], replicated, may hold values from 1 to 4
Outputs:
- state_change: float32 [16, 5, 16, 256, 256], P('inst', None, None, 'blk')
Inputs may be any that keep to these rules, and one draw needn't show every extreme that they name: `state`: density and pressure lie in 0.7 to 1.3, the axial velocity in 0.2 to 0.8 and the other two velocity components in -0.4 to 0.4; the last variable is the total energy p / 0.4 + rho (u u + v v + w w) / 2.
All inputs are finite; a program needn't handle non-finite values.
Results may differ from a plain program's by a relative error of at most 0.0003.
Values sent between devices are 32-bit elements; how exact they have to be, the bound alone decides.
A program may use at most 64 MiB of HBM per device.

v0:
```python
import math

import jax
import jax.numpy as jnp
from jax import lax
from jax.sharding import PartitionSpec as P

NT = 16


heat_ratio = 1.4
segment_step = 0.05
smooth_weight = 0.5
base_rate = 0.5
diagonal_weight = 3.0


def extended_2(cells, sides, width):
    for axis, dim in sides:
        count = lax.axis_size(axis)
        head = lax.slice_in_dim(cells, 0, width, axis=dim)
        tail = lax.slice_in_dim(cells, cells.shape[dim] - width, cells.shape[dim], axis=dim)
        cells = jnp.concatenate(
            [
                lax.ppermute(tail, axis, [(i, (i + 1) % count) for i in range(count)]),
                cells,
                lax.ppermute(head, axis, [((i + 1) % count, i) for i in range(count)]),
            ],
            axis=dim,
        )
    return cells


def limited(lower, upper):
    return jnp.maximum(0.0, jnp.minimum(lower, upper)) + jnp.minimum(0.0, jnp.maximum(lower, upper))


def take_part(array_in, offset, amount, along):
    return lax.slice_in_dim(array_in, offset, offset + amount, axis=along)


def primitive(conserved):
    density = conserved[:, 0]
    velocity = [conserved[:, 1] / density, conserved[:, 2] / density, conserved[:, 3] / density]
    kinetic = (
        0.5
        * density
        * (velocity[0] * velocity[0] + velocity[1] * velocity[1] + velocity[2] * velocity[2])
    )
    pressure = (heat_ratio - 1.0) * (conserved[:, 4] - kinetic)
    return [density] + velocity + [pressure]


def physical(states, normal):
    density = states[0]
    pressure = states[4]
    velocity = states[1:4]
    normal_speed = velocity[normal]
    energy = pressure / (heat_ratio - 1.0) + 0.5 * density * (
        velocity[0] * velocity[0] + velocity[1] * velocity[1] + velocity[2] * velocity[2]
    )
    conserved = [
        density,
        density * velocity[0],
        density * velocity[1],
        density * velocity[2],
        energy,
    ]
    flux = [density * normal_speed]
    for member in range(3):
        momentum = density * normal_speed * velocity[member]
        if member == normal:
            momentum = momentum + pressure
        flux.append(momentum)
    flux.append((energy + pressure) * normal_speed)
    wave_speed = jnp.abs(normal_speed) + jnp.sqrt(heat_ratio * pressure / density)
    return (flux, conserved, wave_speed)


def divergence(states, along, normal):
    extent = states[0].shape[along]
    interior = extent - 4
    left_side = []
    right_side = []
    for component in states:
        differences = take_part(component, 1, extent - 1, along) - take_part(
            component, 0, extent - 1, along
        )
        slopes = limited(
            take_part(differences, 0, interior + 2, along),
            take_part(differences, 1, interior + 2, along),
        )
        centres = take_part(component, 1, interior + 2, along)
        left_side.append(
            take_part(centres, 0, interior + 1, along)
            + 0.5 * take_part(slopes, 0, interior + 1, along)
        )
        right_side.append(
            take_part(centres, 1, interior + 1, along)
            - 0.5 * take_part(slopes, 1, interior + 1, along)
        )
    left_flux, left_cons, left_speed = physical(left_side, normal)
    right_flux, right_cons, right_speed = physical(right_side, normal)
    wave_speed = jnp.maximum(left_speed, right_speed)
    result = []
    for member in range(5):
        face_flux = 0.5 * (left_flux[member] + right_flux[member]) - 0.5 * wave_speed * (
            right_cons[member] - left_cons[member]
        )
        result.append(
            take_part(face_flux, 1, interior, along) - take_part(face_flux, 0, interior, along)
        )
    return result


def residual(extended):
    states = primitive(extended)
    inner = [component[:, :, 2:-2, :] for component in states]
    circum = divergence(states, 2, 1)
    axial = divergence(
        [jnp.pad(component, ((0, 0), (2, 2), (0, 0), (0, 0)), mode="edge") for component in inner],
        1,
        0,
    )
    radial = divergence(
        [jnp.pad(component, ((0, 0), (0, 0), (0, 0), (2, 2)), mode="edge") for component in inner],
        3,
        2,
    )
    return jnp.stack(
        [axial[member] + circum[member] + radial[member] for member in range(5)], axis=1
    )


def transform_tables(instances):
    indices = jnp.arange(instances, dtype=jnp.int32)
    harmonic = jnp.where(indices < 2, indices * (instances // 2), indices // 2)
    phases = harmonic[:, None] * indices[None, :] % instances
    angles = phases.astype(jnp.float32) * (2.0 * math.pi / instances)
    sine_rows = (indices % 2 == 1) & (indices >= 2)
    basis = jnp.where(sine_rows[:, None], jnp.sin(angles), jnp.cos(angles))
    weights = jnp.where(indices < 2, 1.0 / instances, 2.0 / instances).astype(jnp.float32)
    return (basis * weights[:, None], basis.T)


def pair_solve(right, frequency):
    cosine_part = right[:, 0]
    sine_part = right[:, 1]
    determinant = diagonal_weight * diagonal_weight + frequency * frequency
    return jnp.stack(
        [
            (diagonal_weight * cosine_part - frequency * sine_part) / determinant,
            (diagonal_weight * sine_part + frequency * cosine_part) / determinant,
        ],
        axis=1,
    )


def neighbours(extended):
    circum = extended[:, :, :, :, :-2] + extended[:, :, :, :, 2:]
    middle = extended[:, :, :, :, 1:-1]
    padded = jnp.pad(middle, ((0, 0), (0, 0), (0, 0), (0, 0), (0, 0), (1, 1)))
    return circum + (padded[:, :, :, :, :, :-2] + padded[:, :, :, :, :, 2:])


def body(state, multiples):
    extended = extended_2(state, (("blk", 3),), 4)
    first_sweep = residual(extended)
    segmented = extended[:, :, :, 2:-2] - segment_step * first_sweep
    second_sweep = residual(segmented)
    state_freq, residual_freq = (
        lax.all_to_all(state, "inst", split_axis=2, concat_axis=0, tiled=True),
        lax.all_to_all(second_sweep, "inst", split_axis=2, concat_axis=0, tiled=True),
    )
    forward, inverse = transform_tables(NT)
    layout = residual_freq.shape
    paired = (NT // 2, 2) + layout[1:]
    residual_hat = jnp.dot(
        forward, residual_freq.reshape(NT, -1), precision=lax.Precision.HIGHEST
    ).reshape(paired)
    state_hat = jnp.dot(
        forward, state_freq.reshape(NT, -1), precision=lax.Precision.HIGHEST
    ).reshape(paired)
    frequency = jnp.concatenate(
        [jnp.zeros((1,), jnp.float32), base_rate * multiples.astype(jnp.float32)]
    ).reshape(NT // 2, 1, 1, 1, 1)
    source = jnp.stack([frequency * state_hat[:, 1], -frequency * state_hat[:, 0]], axis=1)
    right_hand = -(residual_hat + source)
    widened = extended_2(right_hand, (("blk", 4),), 3)
    correction = pair_solve(widened, frequency)
    for repeat in range(3):
        trimmed = lax.slice_in_dim(widened, repeat + 1, widened.shape[4] - repeat - 1, axis=4)
        correction = pair_solve(trimmed + smooth_weight * neighbours(correction), frequency)
    change_freq = jnp.dot(
        inverse, correction.reshape(NT, -1), precision=lax.Precision.HIGHEST
    ).reshape(layout)
    return lax.all_to_all(change_freq, "inst", split_axis=0, concat_axis=2, tiled=True)


def solution(mesh):
    return jax.shard_map(
        body,
        mesh=mesh,
        in_specs=(P("inst", None, None, "blk", None), P()),
        out_specs=P("inst", None, None, "blk", None),
        check_vma=False,
    )
```

profile of v0, /device:TPU:1, one launch (start us, length us, event | category | flops | bytes accessed | tf_op | source)
XLA Modules:
  0.0 138.5 jit_solution(2675094903121760378)
XLA Ops:
  0.0 1.5 %fusion.215 = (f32[1,5,16,4,256]{4,3,2,1,0:T(4,128)S(1)}, f32[1,5,16,4,256]{4,3,2,1,0:T(4,128)S(1)}) fusion(f32[1,5,16,8,256]{4,3,2,1,0:T(8,128)} %param.2), kind=kLoop, calls=%fused_computation.532 | loop fusion | bytes 1310720 | tf_op jit(solution)/shard_map/slice | solution.py:22
  1.5 6.6 %collective-permute-start = (f32[1,5,16,4,256]{4,3,2,1,0:T(4,128)S(1)}, f32[1,5,16,4,256]{4,3,2,1,0:T(4,128)S(1)}, u32[]{:S(2)}, u32[]{:S(2)}) collective-permute-start(f32[1,5,16,4,256]{4,3,2,1,0:T(4,128)S(1)} %get-tuple-element.83), channel_id=1, source_target_pairs={{0,1},{1,2},{2,3},{3,4},{4,5},{5,6},{6,7},{7,8},{8,9},{9,10},{10,1... | collective-permute-start | bytes 983048 | tf_op jit(solution)/shard_map/ppermute | solution.py:25
  8.1 9.7 %collective-permute-start.1 = (f32[1,5,16,4,256]{4,3,2,1,0:T(4,128)S(1)}, f32[1,5,16,4,256]{4,3,2,1,0:T(4,128)S(1)}, u32[]{:S(2)}, u32[]{:S(2)}) collective-permute-start(f32[1,5,16,4,256]{4,3,2,1,0:T(4,128)S(1)} %get-tuple-element.84), channel_id=1, source_target_pairs={{1,0},{2,1},{3,2},{4,3},{5,4},{6,5},{7,6},{8,7},{9,8},{10,9},{11,1... | collective-permute-start | bytes 983048 | tf_op jit(solution)/shard_map/ppermute | solution.py:27
  17.8 0.9 copy.86
  18.7 6.2 %all-to-all-start.1 = ((f32[1,5,16,8,256]{4,3,1,0,2:T(8,128)}), f32[1,5,16,8,256]{4,3,1,0,2:T(8,128)S(1)}, u32[]{:S(2)}, u32[]{:S(2)}) async-start(f32[1,5,16,8,256]{4,3,1,0,2:T(8,128)} %copy.86), calls=%async_computation.1 | async-start | bytes 1310720 | tf_op jit(solution)/shard_map/all_to_all | solution.py:172
  24.9 4.6 %collective-permute-done = f32[1,5,16,4,256]{4,3,2,1,0:T(4,128)S(1)} collective-permute-done((f32[1,5,16,4,256]{4,3,2,1,0:T(4,128)S(1)}, f32[1,5,16,4,256]{4,3,2,1,0:T(4,128)S(1)}, u32[]{:S(2)}, u32[]{:S(2)}) %collective-permute-start) | collective-permute-done | bytes 327712 | tf_op jit(solution)/shard_map/ppermute | solution.py:25
  37.5 1.4 %multiply_subtract_fusion = (f32[1,16,12,257]{3,2,1,0:T(8,128)S(1)}, f32[1,16,12,257]{3,2,1,0:T(8,128)S(1)}, f32[1,16,12,257]{3,2,1,0:T(8,128)S(1)}, f32[1,16,12,257]{3,2,1,0:T(8,128)S(1)}, f32[1,16,12,257]{3,2,1,0:T(8,128)S(1)}) fusion(f32[1,16,12,258]{3,2,1,0:T(8,128)S(1)} %minimum_add_fusion.1, f32[1,16,12,256]{3,2,1,0:T(8,128)S(1)} %slice.1878, ...), kind=kLoop, calls=%fused_computation.105 | loop fusion | flops 3306048 | bytes 3959040 | tf_op jit(solution)/shard_map/sub | solution.py:107
  42.2 0.9 multiply_subtract_fusion.15
  46.9 1.0 multiply_subtract_fusion.25
  48.7 0.9 multiply_subtract_fusion.28
  61.2 1.6 %copy.101 = f32[1,16,8,1]{2,1,0,3:T(8,128)} copy(f32[1,16,8,1]{3,2,1,0:T(8,128)} %get-tuple-element.103) | data formatting | bytes 1024 | tf_op jit(solution)/shard_map/jit(_pad)/slice | solution.py:126
  62.8 1.6 %copy.102 = f32[1,16,8,1]{2,1,0,3:T(8,128)} copy(f32[1,16,8,1]{3,2,1,0:T(8,128)} %get-tuple-element.104) | data formatting | bytes 1024 | tf_op jit(solution)/shard_map/jit(_pad)/slice | solution.py:126
  69.9 0.9 multiply_subtract_fusion.10
  74.1 0.9 copy.84
  75.1 6.9 %all-to-all-start = ((f32[1,5,16,8,256]{4,3,1,0,2:T(8,128)}), f32[1,5,16,8,256]{4,3,1,0,2:T(8,128)S(1)}, u32[]{:S(2)}, u32[]{:S(2)}) async-start(f32[1,5,16,8,256]{4,3,1,0,2:T(8,128)} %copy.84), calls=%async_computation | async-start | bytes 1310720 | tf_op jit(solution)/shard_map/all_to_all | solution.py:173
  82.4 0.9 convolution_bitcast_fusion.1
  83.5 9.7 %all-to-all-done = f32[1,5,16,8,256]{4,3,1,0,2:T(8,128)S(1)} async-done(((f32[1,5,16,8,256]{4,3,1,0,2:T(8,128)}), f32[1,5,16,8,256]{4,3,1,0,2:T(8,128)S(1)}, u32[]{:S(2)}, u32[]{:S(2)}) %all-to-all-start) | async-done | bytes 655392 | tf_op jit(solution)/shard_map/all_to_all | solution.py:173
  93.5 0.9 fusion.2
  94.4 5.1 %collective-permute-start.2 = (f32[8,2,5,1,3,256]{5,0,4,2,1,3:T(8,128)S(1)}, f32[8,2,5,1,3,256]{5,0,4,2,1,3:T(8,128)S(1)}, u32[]{:S(2)}, u32[]{:S(2)}) collective-permute-start(f32[8,2,5,1,3,256]{5,0,4,2,1,3:T(8,128)S(1)} %get-tuple-element.81), channel_id=1, source_target_pairs={{0,1},{1,2},{2,3},{3,4},{4,5},{5,6},{6,7},{7,8},{8,9},{9,10},{10,1... | collective-permute-start | bytes 737288 | tf_op jit(solution)/shard_map/ppermute | solution.py:25
  99.5 5.3 %collective-permute-start.3 = (f32[8,2,5,1,3,256]{5,0,4,2,1,3:T(8,128)S(1)}, f32[8,2,5,1,3,256]{5,0,4,2,1,3:T(8,128)S(1)}, u32[]{:S(2)}, u32[]{:S(2)}) collective-permute-start(f32[8,2,5,1,3,256]{5,0,4,2,1,3:T(8,128)S(1)} %get-tuple-element.82), channel_id=1, source_target_pairs={{1,0},{2,1},{3,2},{4,3},{5,4},{6,5},{7,6},{8,7},{9,8},{10,9},{11,1... | collective-permute-start | bytes 737288 | tf_op jit(solution)/shard_map/ppermute | solution.py:27
  104.9 7.2 %collective-permute-done.2 = f32[8,2,5,1,3,256]{5,0,4,2,1,3:T(8,128)S(1)} collective-permute-done((f32[8,2,5,1,3,256]{5,0,4,2,1,3:T(8,128)S(1)}, f32[8,2,5,1,3,256]{5,0,4,2,1,3:T(8,128)S(1)}, u32[]{:S(2)}, u32[]{:S(2)}) %collective-permute-start.2) | collective-permute-done | bytes 245792 | tf_op jit(solution)/shard_map/ppermute | solution.py:25
  112.0 4.5 %collective-permute-done.3 = f32[8,2,5,1,3,256]{5,0,4,2,1,3:T(8,128)S(1)} collective-permute-done((f32[8,2,5,1,3,256]{5,0,4,2,1,3:T(8,128)S(1)}, f32[8,2,5,1,3,256]{5,0,4,2,1,3:T(8,128)S(1)}, u32[]{:S(2)}, u32[]{:S(2)}) %collective-permute-start.3) | collective-permute-done | bytes 245792 | tf_op jit(solution)/shard_map/ppermute | solution.py:27
  121.4 16.2 %all_to_all.48 = f32[16,5,1,8,256]{4,3,1,2,0:T(8,128)S(1)} all-to-all(f32[16,5,1,8,256]{4,3,1,2,0:T(8,128)S(1)} %copy.91), channel_id=1, replica_groups=mesh['inst'=16,'blk'=32] {'inst'}, dimensions={0} | all-to-all | bytes 1310720 | tf_op jit(solution)/shard_map/all_to_all | solution.py:197
  137.6 0.9 copy.92
  (283 shorter events, 40.7 us)
Async XLA Ops:
  0.0 17.8 %copy-start = (f32[1,5,16,8,256]{4,3,2,1,0:T(8,128)S(1)}, f32[1,5,16,8,256]{4,3,2,1,0:T(8,128)}, u32[]{:S(2)}) copy-start(f32[1,5,16,8,256]{4,3,2,1,0:T(8,128)} %param.2) | copy-start | bytes 1966084
  1.5 28.0 %collective-permute-start = (f32[1,5,16,4,256]{4,3,2,1,0:T(4,128)S(1)}, f32[1,5,16,4,256]{4,3,2,1,0:T(4,128)S(1)}, u32[]{:S(2)}, u32[]{:S(2)}) collective-permute-start(f32[1,5,16,4,256]{4,3,2,1,0:T(4,128)S(1)} %get-tuple-element.83), channel_id=1, source_target_pairs={{0,1},{1,2},{2,3},{3,4},{4,5},{5,6},{6,7},{7,8},{8,9},{9,10},{10,1... | collective-permute-start | bytes 983048 | tf_op jit(solution)/shard_map/ppermute | solution.py:25
  8.1 21.9 %collective-permute-start.1 = (f32[1,5,16,4,256]{4,3,2,1,0:T(4,128)S(1)}, f32[1,5,16,4,256]{4,3,2,1,0:T(4,128)S(1)}, u32[]{:S(2)}, u32[]{:S(2)}) collective-permute-start(f32[1,5,16,4,256]{4,3,2,1,0:T(4,128)S(1)} %get-tuple-element.84), channel_id=1, source_target_pairs={{1,0},{2,1},{3,2},{4,3},{5,4},{6,5},{7,6},{8,7},{9,8},{10,9},{11,1... | collective-permute-start | bytes 983048 | tf_op jit(solution)/shard_map/ppermute | solution.py:27
  18.7 56.4 %all-to-all-start.1 = ((f32[1,5,16,8,256]{4,3,1,0,2:T(8,128)}), f32[1,5,16,8,256]{4,3,1,0,2:T(8,128)S(1)}, u32[]{:S(2)}, u32[]{:S(2)}) async-start(f32[1,5,16,8,256]{4,3,1,0,2:T(8,128)} %copy.86), calls=%async_computation.1 | async-start | bytes 1310720 | tf_op jit(solution)/shard_map/all_to_all | solution.py:172
  46.7 1.2 copy-start.30
  47.8 1.8 %copy-start.6 = (f32[1,17,8,256]{3,2,1,0:T(8,128)}, f32[1,17,8,256]{3,2,1,0:T(8,128)S(1)}, u32[]{:S(2)}) copy-start(f32[1,17,8,256]{3,2,1,0:T(8,128)S(1)} %get-tuple-element.18) | copy-start | bytes 417796
  47.8 1.8 %copy-start.8 = (f32[1,17,8,256]{3,2,1,0:T(8,128)}, f32[1,17,8,256]{3,2,1,0:T(8,128)S(1)}, u32[]{:S(2)}) copy-start(f32[1,17,8,256]{3,2,1,0:T(8,128)S(1)} %get-tuple-element.19) | copy-start | bytes 417796
  47.8 1.8 %copy-start.10 = (f32[1,17,8,256]{3,2,1,0:T(8,128)}, f32[1,17,8,256]{3,2,1,0:T(8,128)S(1)}, u32[]{:S(2)}) copy-start(f32[1,17,8,256]{3,2,1,0:T(8,128)S(1)} %get-tuple-element.20) | copy-start | bytes 417796
  47.8 1.8 %copy-start.12 = (f32[1,17,8,256]{3,2,1,0:T(8,128)}, f32[1,17,8,256]{3,2,1,0:T(8,128)S(1)}, u32[]{:S(2)}) copy-start(f32[1,17,8,256]{3,2,1,0:T(8,128)S(1)} %get-tuple-element.21) | copy-start | bytes 417796
  64.4 2.1 %copy-start.14 = (f32[1,16,8,258]{3,2,1,0:T(8,128)S(1)}, f32[1,16,8,258]{3,2,1,0:T(8,128)}, u32[]{:S(2)}) copy-start(f32[1,16,8,258]{3,2,1,0:T(8,128)} %minimum_add_fusion.24) | copy-start | bytes 396292
  64.4 2.1 %copy-start.15 = (f32[1,16,8,258]{3,2,1,0:T(8,128)S(1)}, f32[1,16,8,258]{3,2,1,0:T(8,128)}, u32[]{:S(2)}) copy-start(f32[1,16,8,258]{3,2,1,0:T(8,128)} %minimum_add_fusion.23) | copy-start | bytes 396292
  64.4 2.1 %copy-start.21 = (f32[1,16,8,2]{3,2,1,0:T(8,128)S(1)}, f32[1,16,8,2]{3,2,1,0:T(8,128)}, u32[]{:S(2)}) copy-start(f32[1,16,8,2]{3,2,1,0:T(8,128)} %copy-done.20) | copy-start | bytes 3076
  64.4 2.1 %copy-start.23 = (f32[1,16,8,2]{3,2,1,0:T(8,128)S(1)}, f32[1,16,8,2]{3,2,1,0:T(8,128)}, u32[]{:S(2)}) copy-start(f32[1,16,8,2]{3,2,1,0:T(8,128)} %copy-done.22) | copy-start | bytes 3076
  64.4 2.1 %copy-start.25 = (f32[1,16,8,2]{3,2,1,0:T(8,128)S(1)}, f32[1,16,8,2]{3,2,1,0:T(8,128)}, u32[]{:S(2)}) copy-start(f32[1,16,8,2]{3,2,1,0:T(8,128)} %copy-done.24) | copy-start | bytes 3076
  64.5 2.1 %copy-start.27 = (f32[1,16,8,2]{3,2,1,0:T(8,128)S(1)}, f32[1,16,8,2]{3,2,1,0:T(8,128)}, u32[]{:S(2)}) copy-start(f32[1,16,8,2]{3,2,1,0:T(8,128)} %copy-done.26) | copy-start | bytes 3076
  64.5 2.1 %copy-start.29 = (f32[1,16,8,2]{3,2,1,0:T(8,128)S(1)}, f32[1,16,8,2]{3,2,1,0:T(8,128)}, u32[]{:S(2)}) copy-start(f32[1,16,8,2]{3,2,1,0:T(8,128)} %copy-done.28) | copy-start | bytes 3076
  67.8 1.1 copy-start.3
  72.0 1.1 copy-start.11
  72.0 1.1 copy-start.13
  72.0 1.1 copy-start.31
  74.1 7.8 %copy-start.32 = (s32[7]{0:T(128)S(1)}, s32[7]{0:T(128)}, u32[]{:S(2)}) copy-start(s32[7]{0:T(128)} %param.3) | copy-start | bytes 88
  75.1 18.1 %all-to-all-start = ((f32[1,5,16,8,256]{4,3,1,0,2:T(8,128)}), f32[1,5,16,8,256]{4,3,1,0,2:T(8,128)S(1)}, u32[]{:S(2)}, u32[]{:S(2)}) async-start(f32[1,5,16,8,256]{4,3,1,0,2:T(8,128)} %copy.84), calls=%async_computation | async-start | bytes 1310720 | tf_op jit(solution)/shard_map/all_to_all | solution.py:173
  94.4 17.6 %collective-permute-start.2 = (f32[8,2,5,1,3,256]{5,0,4,2,1,3:T(8,128)S(1)}, f32[8,2,5,1,3,256]{5,0,4,2,1,3:T(8,128)S(1)}, u32[]{:S(2)}, u32[]{:S(2)}) collective-permute-start(f32[8,2,5,1,3,256]{5,0,4,2,1,3:T(8,128)S(1)} %get-tuple-element.81), channel_id=1, source_target_pairs={{0,1},{1,2},{2,3},{3,4},{4,5},{5,6},{6,7},{7,8},{8,9},{9,10},{10,1... | collective-permute-start | bytes 737288 | tf_op jit(solution)/shard_map/ppermute | solution.py:25
  99.5 17.0 %collective-permute-start.3 = (f32[8,2,5,1,3,256]{5,0,4,2,1,3:T(8,128)S(1)}, f32[8,2,5,1,3,256]{5,0,4,2,1,3:T(8,128)S(1)}, u32[]{:S(2)}, u32[]{:S(2)}) collective-permute-start(f32[8,2,5,1,3,256]{5,0,4,2,1,3:T(8,128)S(1)} %get-tuple-element.82), channel_id=1, source_target_pairs={{1,0},{2,1},{3,2},{4,3},{5,4},{6,5},{7,6},{8,7},{9,8},{10,9},{11,1... | collective-permute-start | bytes 737288 | tf_op jit(solution)/shard_map/ppermute | solution.py:27
  (15 other events, 12.9 us)
where the time goes:
time: 140 us; the launch traced here: 138 us
  starting transfers between devices  39.8 us (28%)
  other arithmetic  30.4 us (22%)
  waiting for transfers between devices  26.5 us (19%)
  local copies, waits for them, and re-layouts  21.4 us (15%)
  blocking collectives  16.2 us (12%)
  matrix products  2.6 us (2%)
  between operations  1.65 us (1%)
    all_to_all x1, blocking collectives, body(): lax.all_to_all(change_freq, 'inst', split_axis=0, concat_axis=2, tiled=True)  16.2 us
    ppermute x2, starting transfers between devices, extended_2(): lax.ppermute(head, axis, [((i + 1) % count, i) for i in range(count)])  15 us
    sub x20, other arithmetic, divergence(): 0.5 * (left_flux[member] + right_flux[member])  13.7 us
    ppermute x2, waiting for transfers between devices, extended_2(): lax.ppermute(tail, axis, [(i, (i + 1) % count) for i in range(count)])  11.8 us
    ppermute x2, starting transfers between devices, extended_2(): lax.ppermute(tail, axis, [(i, (i + 1) % count) for i in range(count)])  11.7 us
    all_to_all x1, waiting for transfers between devices, body(): lax.all_to_all(second_sweep, 'inst', split_axis=2, concat_axis=0, tiled=T...  9.7 us
    unnamed x70, local copies, waits for them, and re-layouts  7.32 us
    all_to_all x1, starting transfers between devices, body(): lax.all_to_all(second_sweep, 'inst', split_axis=2, concat_axis=0, tiled=T...  6.87 us
  transfers between devices with their start and end apart: 6, of which 5 were waited for; matrix products, arithmetic and copies ran while one was open for 29% of the time, Pallas kernels for 0%

commit v1 on v0

v1 whole, which is shorter than its diff:
```python
import functools
import math

import jax
import jax.numpy as jnp
from jax import lax
from jax.experimental import pallas as pl
from jax.experimental.pallas import tpu as pltpu
from jax.sharding import PartitionSpec as P

NI = 16
NB = 32
MESH = pl.DeviceIdType.MESH
GROUPS = ((0,), (1,), (2,), (3,), (4,))
SOUND = math.sqrt(1.4)
C1 = math.cos(math.pi / 8)
C2 = math.sqrt(0.5)
C3 = math.sin(math.pi / 8)
OFFSETS = tuple(
    (z, x, c) for z in (1, 0) for x in (2, 1, 3, 0) for c in (1, 0) if (z, x, c) != (0, 0, 0)
)


def primitive(s):
    inv = 1.0 / s[0]
    u, v, w = s[1] * inv, s[2] * inv, s[3] * inv
    p = 0.4 * s[4] - 0.2 * (s[1] * u + s[2] * v + s[3] * w)
    return [s[0], u, v, w, p]


def face2(left, right, normal):
    def sound(q):
        t = q[0] * q[4]
        return (SOUND * q[4]) * lax.rsqrt(jnp.maximum(t, 1e-30))

    unl, unr = left[1 + normal], right[1 + normal]
    a = jnp.maximum(jnp.abs(unl) + sound(left), jnp.abs(unr) + sound(right))
    ml, mr = unl + a, unr - a
    gl, gr = left[0] * ml, right[0] * mr
    out = [gl + gr]
    kl = kr = None
    for m in range(3):
        fl, fr = gl * left[1 + m], gr * right[1 + m]
        flux = fl + fr
        if m == normal:
            flux = flux + (left[4] + right[4])
        out.append(flux)
        tl, tr = fl * left[1 + m], fr * right[1 + m]
        kl = tl if kl is None else kl + tl
        kr = tr if kr is None else kr + tr
    out.append(
        0.5 * (kl + kr)
        + (left[4] * (2.5 * ml + unl) + right[4] * (2.5 * mr + unr))
    )
    return out


def cell2(q, normal):
    un = q[1 + normal]
    half = q[0] * un
    g = half + half
    out = [g]
    for m in range(3):
        flux = g * q[1 + m]
        if m == normal:
            flux = flux + (q[4] + q[4])
        out.append(flux)
    out.append(half * (q[1] * q[1] + q[2] * q[2] + q[3] * q[3]) + 7.0 * q[4] * un)
    return out


def half_slope(a, b):
    return 0.5 * jnp.maximum(jnp.minimum(a, b), jnp.minimum(jnp.maximum(a, b), 0.0))


def shift_next(lo, hi, edge, axis):
    size = lo.shape[axis]
    last = lax.broadcasted_iota(jnp.int32, lo.shape, axis) == size - 1
    rl, rh = pltpu.roll(lo, size - 1, axis), pltpu.roll(hi, size - 1, axis)
    return jnp.where(last, rh, rl), jnp.where(last, edge, rh)


def shift_prev(lo, hi, edge, axis):
    first = lax.broadcasted_iota(jnp.int32, lo.shape, axis) == 0
    rl, rh = pltpu.roll(lo, 1, axis), pltpu.roll(hi, 1, axis)
    return jnp.where(first, edge, rl), jnp.where(first, rl, rh)


def line_div(lo, hi, normal, axis):
    left_lo, left_hi, right_lo, right_hi = [], [], [], []
    for v in range(5):
        a, b = lo[v], hi[v]
        na, nb = shift_next(a, b, b, axis)
        da, db = na - a, nb - b
        pa, pb = shift_prev(da, db, 0.0, axis)
        ha, hb = half_slope(pa, da), half_slope(pb, db)
        left_lo.append(a + ha)
        left_hi.append(b + hb)
        ra, rb = shift_next(a - ha, b - hb, b, axis)
        right_lo.append(ra)
        right_hi.append(rb)
    f_lo = face2(left_lo, right_lo, normal)
    f_hi = face2(left_hi, right_hi, normal)
    edge = cell2(lo, normal)
    out_lo, out_hi = [], []
    for v in range(5):
        a, b = shift_prev(f_lo[v], f_hi[v], edge[v], axis)
        out_lo.append(f_lo[v] - a)
        out_hi.append(f_hi[v] - b)
    return out_lo, out_hi


def axial_radial(prim, acc, r):
    q = [[prim[r, v, c] for v in range(5)] for c in range(4)]
    total = [None] * 4
    for c0, c1, normal, axis in ((0, 1, 2, 1), (2, 3, 2, 1), (0, 2, 0, 0), (1, 3, 0, 0)):
        lo, hi = line_div(q[c0], q[c1], normal, axis)
        for c, part in ((c0, lo), (c1, hi)):
            total[c] = part if total[c] is None else [s + t for s, t in zip(total[c], part)]
    for c in range(4):
        for v in range(5):
            acc[r, v, c] = total[c][v]


def column(prim, c, first, last, emit, before=None, after=None):
    lo = first - 2 if before is None else first - 1
    hi = last + 2 if after is None else last + 1
    w = {r: [prim[r, v, c] for v in range(5)] for r in range(lo, hi + 1)}
    d = {r: [w[r + 1][v] - w[r][v] for v in range(5)] for r in range(lo, hi)}
    h = {
        r: [half_slope(d[r - 1][v], d[r][v]) for v in range(5)] for r in range(lo + 1, hi)
    }

    def flux(r):
        return face2(
            [w[r][v] + h[r][v] for v in range(5)],
            [w[r + 1][v] - h[r + 1][v] for v in range(5)],
            1,
        )

    low = previous = flux(first - 1) if before is None else before
    for r in range(first, last + 1):
        face = after if r == last and after is not None else flux(r)
        emit(r, [face[v] - previous[v] for v in range(5)])
        previous = face
    return low, previous


def kernel(
    multiples, state, out,
    cons, prim, acc, edges, prim2, acc2,
    state_in, sweep_out, sweep_in, table, source,
    rhs, corr, last_corr, change,
    halo_send, halo_recv, state_send, state_recv, sweep_send, sweep_recv,
    rhs_send, rhs_recv, change_send, change_recv,
):
    me = lax.axis_index("inst")
    blk = lax.axis_index("blk")
    up, down = lax.rem(blk + 1, NB), lax.rem(blk + NB - 1, NB)
    my_core = lax.rem(me, 2)
    my_x = lax.rem(me // 2, 4)
    my_z = me // 8

    def peer(offset):
        z, x, c = offset
        return lax.rem(my_z + z, 2) * 8 + lax.rem(my_x + x, 4) * 2 + lax.rem(my_core + c, 2)

    barrier = pltpu.get_barrier_semaphore()
    for there in (up, down):
        pl.semaphore_signal(barrier, inc=1, device_id=(me, there), device_id_type=MESH)
    for offset in OFFSETS:
        pl.semaphore_signal(barrier, inc=1, device_id=(peer(offset), blk), device_id_type=MESH)

    for y in range(8):
        for c in range(4):
            rows = pl.ds((c // 2) * 64 + y, 8, stride=8)
            s = [state[v, c % 2, rows, :] for v in range(5)]
            q = primitive(s)
            for v in range(5):
                cons[y + 4, v, c] = s[v]
                prim[y + 4, v, c] = q[v]

    pl.semaphore_wait(barrier, NI - 1 + 2)

    def remote(source_ref, target_ref, send, recv, there):
        return pltpu.make_async_remote_copy(
            src_ref=source_ref, dst_ref=target_ref, send_sem=send, recv_sem=recv,
            device_id=there, device_id_type=MESH,
        )

    halos = []
    for k, (mine, theirs, there) in enumerate(
        ((4, 12, down), (10, 2, up), (6, 14, down), (8, 0, up))
    ):
        halos.append(
            remote(
                cons.at[pl.ds(mine, 2)], cons.at[pl.ds(theirs, 2)],
                halo_send.at[k], halo_recv.at[k], (me, there),
            )
        )
        halos[-1].start()

    for k in range(8):
        rate = 0.0 if k == 0 else 0.5 * multiples[k - 1].astype(jnp.float32)
        rate = jnp.full((8, 128), rate, jnp.float32)
        det = 9.0 + rate * rate
        table[0, k] = 3.0 / det
        table[1, k] = rate / det
        table[2, k] = rate * 0.125

    def own_axial_radial(r, carry):
        axial_radial(prim, acc, r)
        return carry

    lax.fori_loop(4, 12, own_axial_radial, 0)

    def halo_primitive(r):
        for c in range(4):
            q = primitive([cons[r, v, c] for v in range(5)])
            for v in range(5):
                prim[r, v, c] = q[v]

    halos[0].wait_recv()
    halos[1].wait_recv()
    for r in (2, 3, 12, 13):
        halo_primitive(r)

    def segment(c):
        def emit(r, diff):
            s = [cons[r, v, c] - 0.025 * (acc[r, v, c] + diff[v]) for v in range(5)]
            q = primitive(s)
            for v in range(5):
                prim2[r, v, c] = q[v]

        return emit

    def own_column(c, carry):
        low, high = column(prim, c, 4, 11, segment(c))
        for v in range(5):
            edges[0, v, c] = low[v]
            edges[1, v, c] = high[v]
        return carry

    lax.fori_loop(0, 4, own_column, 0)

    states = []
    for k, offset in enumerate(OFFSETS):
        t = peer(offset)
        states.append(
            remote(
                state.at[:, :, pl.ds(pl.multiple_of(8 * t, 8), 8), :], state_in.at[me],
                state_send.at[k], state_recv.at[k], (t, blk),
            )
        )
        states[-1].start()

    def sweep2_axial_radial(r, carry):
        axial_radial(prim2, acc2, r)
        return carry

    def halo_axial_radial(k, carry):
        axial_radial(prim, acc, k + 2 + 8 * (k // 2))
        return carry

    lax.fori_loop(0, 4, halo_axial_radial, 0)
    lax.fori_loop(4, 12, sweep2_axial_radial, 0)

    halos[2].wait_recv()
    halos[3].wait_recv()
    for r in (0, 1, 14, 15):
        halo_primitive(r)

    def halo_column(c, carry):
        column(prim, c, 2, 3, segment(c), after=[edges[0, v, c] for v in range(5)])
        column(prim, c, 12, 13, segment(c), before=[edges[1, v, c] for v in range(5)])
        return carry

    lax.fori_loop(0, 4, halo_column, 0)

    def sweep2_column(c, carry):
        xh, zh = c // 2, lax.rem(c, 2)

        def emit(r, diff):
            for v in range(5):
                rows = pl.ds(xh * 640 + v * 16 + zh * 8 + (r - 4), 8, stride=80)
                sweep_out[rows, :] = acc2[r, v, c] + diff[v]

        column(prim2, c, 4, 11, emit)
        return carry

    lax.fori_loop(0, 4, sweep2_column, 0)

    sweeps = []
    for g, group in enumerate(GROUPS):
        first, rows = 16 * group[0], 16 * len(group)
        sweeps.append([])
        for k, offset in enumerate(OFFSETS):
            t = peer(offset)
            sweeps[g].append(
                remote(
                    sweep_out.at[pl.ds(pl.multiple_of(80 * t + first, 8), rows)],
                    sweep_in.at[me, pl.ds(first, rows)],
                    sweep_send.at[g, k], sweep_recv.at[g, k], (t, blk),
                )
            )
            sweeps[g][-1].start()
    for v in range(5):
        for zh in range(2):
            state_in[me, v, zh] = state[v, zh, pl.ds(pl.multiple_of(8 * me, 8), 8), :]
    own = sweep_out[pl.ds(pl.multiple_of(80 * me, 8), 80), :]
    sweep_in[me] = own

    for copy in states:
        copy.wait_recv()

    def solve(k, a, b):
        alpha, beta = table[0, k], table[1, k]
        return alpha * a - beta * b, alpha * b + beta * a

    def source_of(v, carry):
        for zh in range(2):
            x = forward([state_in[n, v, zh] for n in range(NI)])
            for k in range(1, 8):
                scale = table[2, k]
                a, b = solve(k, -(scale * x[2 * k + 1]), scale * x[2 * k])
                source[v, zh, 2 * k] = a
                source[v, zh, 2 * k + 1] = b
        return carry

    lax.fori_loop(0, 5, source_of, 0)

    rhs_copies = []
    for g, group in enumerate(GROUPS):
        for copy in sweeps[g]:
            copy.wait_recv()

        def right_hand(v, carry):
            for zh in range(2):
                first = pl.multiple_of(v * 16 + zh * 8, 8)
                x = forward([sweep_in[n, pl.ds(first, 8), :] for n in range(NI)])
                for k in range(8):
                    if k == 0:
                        a, b = x[0] * (-1.0 / 96.0), x[1] * (-1.0 / 96.0)
                    else:
                        a, b = solve(k, x[2 * k] * (-0.0625), x[2 * k + 1] * (-0.0625))
                        a = a + source[v, zh, 2 * k]
                        b = b + source[v, zh, 2 * k + 1]
                    rhs[v, zh, pl.ds(3 * 16 + k, 8, stride=16), :] = a
                    rhs[v, zh, pl.ds(3 * 16 + 8 + k, 8, stride=16), :] = b
            return carry

        lax.fori_loop(group[0], group[-1] + 1, right_hand, 0)
        vs = pl.ds(group[0], len(group))
        pair = []
        for k, (mine, theirs, there) in enumerate(((3, 11, down), (8, 0, up))):
            pair.append(
                remote(
                    rhs.at[vs, :, pl.ds(16 * mine, 48), :], rhs.at[vs, :, pl.ds(16 * theirs, 48), :],
                    rhs_send.at[g, k], rhs_recv.at[g, k], (me, there),
                )
            )
            pair[-1].start()
        rhs_copies.append(pair)

    pair_index = lax.broadcasted_iota(jnp.int32, (8, 128), 0)
    rate = jnp.zeros((8, 128), jnp.float32)
    for k in range(1, 8):
        rate = jnp.where(pair_index == k, 0.5 * multiples[k - 1].astype(jnp.float32), rate)
    det = 9.0 + rate * rate
    alpha, beta = 1.5 / det, (0.5 * rate) / det

    changes = []
    for g, group in enumerate(GROUPS):
        for copy in rhs_copies[g]:
            copy.wait_recv()

        def smooth(v, carry):
            def at(ref, row, ab, zh, shift=0):
                return ref[v, zh, pl.ds(16 * (row - shift) + 8 * ab, 8), :]

            def step(src, dst, first, last, src_shift=0, dst_shift=0):
                for row in range(first, last + 1):
                    nb = []
                    for ab in range(2):
                        lo, hi = (at(src, row, ab, zh, src_shift) for zh in range(2))
                        nlo, nhi = shift_next(lo, hi, 0.0, 1)
                        plo, phi = shift_prev(lo, hi, 0.0, 1)
                        both = []
                        for zh, t in ((0, nlo + plo), (1, nhi + phi)):
                            y = at(src, row - 1, ab, zh, src_shift) + at(src, row + 1, ab, zh, src_shift)
                            both.append(y + t)
                        nb.append(both)
                    for zh in range(2):
                        a, b = nb[0][zh], nb[1][zh]
                        for ab, t in ((0, alpha * a - beta * b), (1, alpha * b + beta * a)):
                            dst[v, zh, pl.ds(16 * (row - dst_shift) + 8 * ab, 8), :] = (
                                at(rhs, row, ab, zh) + t
                            )

            step(rhs, corr.at[0], 1, 12)
            step(corr.at[0], corr.at[1], 2, 11)
            step(corr.at[1], last_corr, 3, 10, 0, 3)
            for zh in range(2):
                c = [
                    last_corr[v, zh, pl.ds(8 * ab + k, 8, stride=16), :]
                    for k in range(8)
                    for ab in range(2)
                ]
                x = backward(c)
                for n in range(NI):
                    change[n, v, zh] = x[n]
            return carry

        lax.fori_loop(group[0], group[-1] + 1, smooth, 0)
        vs = pl.ds(group[0], len(group))
        changes.append([])
        here = pl.ds(pl.multiple_of(8 * me, 8), 8)
        for k, offset in enumerate(OFFSETS):
            t = peer(offset)
            changes[g].append(
                remote(
                    change.at[t, vs], out.at[vs, :, here, :],
                    change_send.at[g, k], change_recv.at[g, k], (t, blk),
                )
            )
            changes[g][-1].start()
        for v in group:
            for zh in range(2):
                out[v, zh, here, :] = change[me, v, zh]

    for copies in [halos, states] + sweeps + rhs_copies:
        for copy in copies:
            copy.wait_send()
    for copies in changes:
        for copy in copies:
            copy.wait()


def forward(x):
    e = [x[n] + x[n + 8] for n in range(8)]
    o = [x[n] - x[n + 8] for n in range(8)]
    ee = [e[n] + e[n + 4] for n in range(4)]
    eo = [e[n] - e[n + 4] for n in range(4)]
    out = [None] * 16
    s, t = ee[0] + ee[2], ee[1] + ee[3]
    out[0], out[1] = s + t, s - t
    out[8], out[9] = ee[0] - ee[2], ee[1] - ee[3]
    s, t = C2 * (eo[1] - eo[3]), C2 * (eo[1] + eo[3])
    out[4], out[5] = eo[0] + s, t + eo[2]
    out[12], out[13] = eo[0] - s, t - eo[2]
    p = [o[n] - o[8 - n] for n in range(1, 4)]
    q = [o[n] + o[8 - n] for n in range(1, 4)]
    m = C2 * p[1]
    s, t = o[0] + m, o[0] - m
    y, z = C1 * p[0] + C3 * p[2], C3 * p[0] - C1 * p[2]
    out[2], out[14] = s + y, s - y
    out[6], out[10] = t + z, t - z
    m = C2 * q[1]
    s, t = m + o[4], m - o[4]
    y, z = C3 * q[0] + C1 * q[2], C1 * q[0] - C3 * q[2]
    out[3], out[15] = y + s, y - s
    out[7], out[11] = z + t, z - t
    return out


def backward(c):
    s, t = c[0] + c[1], c[0] - c[1]
    ee = [s + c[8], t + c[9], s - c[8], t - c[9]]
    y, z = C2 * (c[4] - c[12]), C2 * (c[5] + c[13])
    eo = [c[4] + c[12], z + y, c[5] - c[13], z - y]
    e = [ee[n] + eo[n] for n in range(4)] + [ee[n] - eo[n] for n in range(4)]
    s, d = c[2] + c[14], c[2] - c[14]
    t, g = c[6] + c[10], c[6] - c[10]
    p = [None, C1 * d + C3 * g, C2 * (s - t), C3 * d - C1 * g]
    o0 = s + t
    s, d = c[3] + c[15], c[3] - c[15]
    t, g = c[7] + c[11], c[7] - c[11]
    q = [None, C3 * s + C1 * t, C2 * (d + g), C1 * s - C3 * t]
    o4 = d - g
    o = [o0] + [q[n] + p[n] for n in range(1, 4)] + [o4]
    o += [q[n] - p[n] for n in (3, 2, 1)]
    return [e[n] + o[n] for n in range(8)] + [e[n] - o[n] for n in range(8)]


def body(state, multiples):
    f32 = jnp.float32
    tiles = lambda rows: pltpu.VMEM((rows, 5, 4, 8, 128), f32)
    peers = len(OFFSETS)
    groups = len(GROUPS)
    dma = pltpu.SemaphoreType.DMA
    halves = state.reshape(5, 128, 2, 128).transpose(0, 2, 1, 3)
    change = pl.pallas_call(
        kernel,
        out_shape=jax.ShapeDtypeStruct((5, 2, 128, 128), f32),
        in_specs=[
            pl.BlockSpec(memory_space=pltpu.SMEM),
            pl.BlockSpec(memory_space=pltpu.VMEM),
        ],
        out_specs=pl.BlockSpec(memory_space=pltpu.VMEM),
        scratch_shapes=[
            tiles(16), tiles(16), tiles(16),
            pltpu.VMEM((2, 5, 4, 8, 128), f32),
            tiles(16), tiles(16),
            pltpu.VMEM((NI, 5, 2, 8, 128), f32),
            pltpu.VMEM((NI * 80, 128), f32),
            pltpu.VMEM((NI, 80, 128), f32),
            pltpu.VMEM((3, 8, 8, 128), f32),
            pltpu.VMEM((5, 2, 16, 8, 128), f32),
            pltpu.VMEM((5, 2, 14 * 16, 128), f32),
            pltpu.VMEM((2, 5, 2, 14 * 16, 128), f32),
            pltpu.VMEM((5, 2, 8 * 16, 128), f32),
            pltpu.VMEM((NI, 5, 2, 8, 128), f32),
            dma((4,)), dma((4,)),
            dma((peers,)), dma((peers,)),
            dma((groups, peers)), dma((groups, peers)),
            dma((groups, 2)), dma((groups, 2)),
            dma((groups, peers)), dma((groups, peers)),
        ],
        compiler_params=pltpu.CompilerParams(
            collective_id=0, has_side_effects=True, vmem_limit_bytes=40 * 2**20
        ),
    )(multiples, halves)
    return change.transpose(0, 2, 1, 3).reshape(state.shape)


def solution(mesh):
    return jax.shard_map(
        body,
        mesh=mesh,
        in_specs=(P("inst", None, None, "blk", None), P()),
        out_specs=P("inst", None, None, "blk", None),
        check_vma=False,
    )
```

time: 140 us -> 74.9 us (0.54)
  Pallas kernels: 0 us -> 70.8 us
  starting transfers between devices: 39.8 us -> 0 us
  other arithmetic: 30.4 us -> 0 us
  waiting for transfers between devices: 26.5 us -> 0 us
  local copies, waits for them, and re-layouts: 21.4 us -> 3.98 us
  blocking collectives: 16.2 us -> 0 us
  matrix products: 2.6 us -> 0 us
  between operations: 1.65 us -> 0.04 us
    pallas_call x0 -> x1, Pallas kernels: none -> 70.8 us  [body(): pl.pallas_call(kernel, out_shape=jax.ShapeDtypeStruct((5, 2, 128, 128), f...]
    ppermute x4 -> x0, starting transfers between devices: 26.7 us -> none  [the longest x2 15 us: extended_2(): lax.ppermute(head, axis, [((i + 1) % count, i) for i in range(count)])]
    sub x49 -> x0, other arithmetic: 19.5 us -> none  [the longest x20 13.7 us: divergence(): 0.5 * (left_flux[member] + right_flux[member])]
    ppermute x4 -> x0, waiting for transfers between devices: 16.8 us -> none  [the longest x2 11.8 us: extended_2(): lax.ppermute(tail, axis, [(i, (i + 1) % count) for i in range(count)])]
    all_to_all x1 -> x0, blocking collectives: 16.2 us -> none  [body(): lax.all_to_all(change_freq, 'inst', split_axis=0, concat_axis=2, tiled=True)]
    all_to_all x2 -> x0, starting transfers between devices: 13 us -> none  [the longest x1 6.87 us: body(): lax.all_to_all(second_sweep, 'inst', split_axis=2, concat_axis=0, tiled=T...]
    all_to_all x2 -> x0, waiting for transfers between devices: 9.7 us -> none  [the longest x1 9.7 us: body(): lax.all_to_all(second_sweep, 'inst', split_axis=2, concat_axis=0, tiled=T...]
    slice x38 -> x0, local copies, waits for them, and re-layouts: 8.05 us -> none  [the longest x18 6.29 us: residual(): jnp.pad(component, ((0, 0), (0, 0), (0, 0), (2, 2)), mode='edge')]
  transfers between devices with their start and end apart: 6 -> 0, of which waited for: 5 -> 0; matrix products, arithmetic and copies ran while one was open for 29% -> 0% of each run, Pallas kernels for 0% -> 0%
where the time goes in v1:
time: 74.9 us; the launch traced here: 74.8 us
  Pallas kernels  70.8 us (95%)
  local copies, waits for them, and re-layouts  3.98 us (5%)
    pallas_call x1, Pallas kernels, body(): pl.pallas_call(kernel, out_shape=jax.ShapeDtypeStruct((5, 2, 128, 128), f...  70.8 us

profile of v1, /device:TPU:1, one launch (start us, length us, event | category | flops | bytes accessed | tf_op | source)
XLA Modules:
  0.0 74.8 jit_solution(8174305614942817701)
XLA Ops:
  0.0 1.4 %reshape.6 = f32[5,128,2,128]{3,2,1,0:T(2,128)S(1)} reshape(f32[1,5,16,8,256]{4,3,2,1,0:T(8,128)} %param.2) | data formatting | bytes 1310720 | tf_op jit(solution)/shard_map/reshape | solution.py:491
  1.5 0.0 copy-start
  1.5 0.6 copy-done
  2.1 70.8 %shard_map.28 = f32[5,2,128,128]{3,2,1,0:T(8,128)S(1)} custom-call(s32[7]{0:T(128)S(1)} %copy-done, f32[5,2,128,128]{3,2,1,0:T(8,128)S(1)} %bitcast.6), custom_call_target="tpu_custom_call" | custom-call | tf_op jit(solution)/shard_map/pallas_call | solution.py:492
  72.9 0.5 copy.4
  73.4 1.4 %reshape.7 = f32[1,5,16,8,256]{4,3,2,1,0:T(8,128)} reshape(f32[5,128,2,128]{3,2,1,0:T(2,128)S(1)} %copy.4) | data formatting | bytes 1310720 | tf_op jit(solution)/shard_map/reshape | solution.py:523
  (1 shorter events, 0.0 us)
Async XLA Ops:
  1.5 0.7 copy-start

commit v2 on v1

--- a/solution.py
+++ b/solution.py
@@ -147,11 +147,11 @@
 
 
 def kernel(
-    multiples, state, out,
-    cons, prim, acc, edges, prim2, acc2,
-    state_in, sweep_out, sweep_in, table, source,
+    multiples_hbm, state_hbm, out,
+    multiples, state, cons, prim, acc, edges, prim2, acc2,
+    state_out, state_in, relay_out, sweep_out, sweep_in, table, source,
     rhs, corr, last_corr, change,
-    halo_send, halo_recv, state_send, state_recv, sweep_send, sweep_recv,
+    load_sem, halo_send, halo_recv, state_send, state_recv, relay_send, relay_recv, sweep_send, sweep_recv,
     rhs_send, rhs_recv, change_send, change_recv,
 ):
     me = lax.axis_index("inst")
@@ -165,22 +165,43 @@
         z, x, c = offset
         return lax.rem(my_z + z, 2) * 8 + lax.rem(my_x + x, 4) * 2 + lax.rem(my_core + c, 2)
 
+    relay_blk = lax.rem(blk + NB - 1 + 2 * my_z, NB)
+    other_z = 1 - my_z
+
     barrier = pltpu.get_barrier_semaphore()
     for there in (up, down):
         pl.semaphore_signal(barrier, inc=1, device_id=(me, there), device_id_type=MESH)
     for offset in OFFSETS:
         pl.semaphore_signal(barrier, inc=1, device_id=(peer(offset), blk), device_id_type=MESH)
+        if offset[0] == 1:
+            pl.semaphore_signal(
+                barrier, inc=1, device_id=(peer(offset), relay_blk), device_id_type=MESH
+            )
+
+    loads = [
+        pltpu.make_async_copy(
+            state_hbm.at[:, :, pl.ds(128 * zh, 128)], state.at[zh], load_sem.at[zh]
+        )
+        for zh in range(2)
+    ]
+    loads.append(pltpu.make_async_copy(multiples_hbm, multiples, load_sem.at[2]))
+    for copy in loads:
+        copy.start()
+    for copy in loads:
+        copy.wait()
 
     for y in range(8):
         for c in range(4):
             rows = pl.ds((c // 2) * 64 + y, 8, stride=8)
-            s = [state[v, c % 2, rows, :] for v in range(5)]
+            s = [state[c % 2, v, rows, :] for v in range(5)]
             q = primitive(s)
             for v in range(5):
                 cons[y + 4, v, c] = s[v]
                 prim[y + 4, v, c] = q[v]
-
-    pl.semaphore_wait(barrier, NI - 1 + 2)
+                row = (c // 2) * 640 + (y // 4) * 40 + v * 8 + (c % 2) * 4 + y % 4
+                state_out[pl.ds(row, 8, stride=80), :] = s[v]
+
+    pl.semaphore_wait(barrier, NI - 1 + 2 + 8)
 
     def remote(source_ref, target_ref, send, recv, there):
         return pltpu.make_async_remote_copy(
@@ -243,30 +264,40 @@
 
     lax.fori_loop(0, 4, own_column, 0)
 
+    def sweep2_axial_radial(r, carry):
+        axial_radial(prim2, acc2, r)
+        return carry
+
+    def halo_axial_radial(k, carry):
+        axial_radial(prim, acc, k + 2 + 8 * (k // 2))
+        return carry
+
+    lax.fori_loop(0, 4, halo_axial_radial, 0)
+    lax.fori_loop(4, 12, sweep2_axial_radial, 0)
+
     states = []
     for k, offset in enumerate(OFFSETS):
         t = peer(offset)
+        first, rows = (0, 80) if offset[0] == 0 else (pl.multiple_of(40 * my_z, 8), 40)
         states.append(
             remote(
-                state.at[:, :, pl.ds(pl.multiple_of(8 * t, 8), 8), :], state_in.at[me],
+                state_out.at[pl.ds(pl.multiple_of(80 * t + first, 8), rows)],
+                state_in.at[me, pl.ds(first, rows)],
                 state_send.at[k], state_recv.at[k], (t, blk),
             )
         )
         states[-1].start()
-
-    def sweep2_axial_radial(r, carry):
-        axial_radial(prim2, acc2, r)
-        return carry
-
-    def halo_axial_radial(k, carry):
-        axial_radial(prim, acc, k + 2 + 8 * (k // 2))
-        return carry
-
-    lax.fori_loop(0, 4, halo_axial_radial, 0)
-    lax.fori_loop(4, 12, sweep2_axial_radial, 0)
+    own = state_out[pl.ds(pl.multiple_of(80 * me, 8), 80), :]
+    state_in[me] = own
 
     halos[2].wait_recv()
     halos[3].wait_recv()
+    for y in range(4):
+        for v in range(5):
+            for zh in range(2):
+                relay_out[pl.ds(v * 8 + zh * 4 + y, 8, stride=40), :] = cons[
+                    12 * my_z + y, v, 2 * other_z + zh
+                ]
     for r in (0, 1, 14, 15):
         halo_primitive(r)
 
@@ -304,13 +335,23 @@
                 )
             )
             sweeps[g][-1].start()
-    for v in range(5):
-        for zh in range(2):
-            state_in[me, v, zh] = state[v, zh, pl.ds(pl.multiple_of(8 * me, 8), 8), :]
     own = sweep_out[pl.ds(pl.multiple_of(80 * me, 8), 80), :]
     sweep_in[me] = own
 
-    for copy in states:
+    relays = []
+    for k, offset in enumerate(OFFSETS):
+        if offset[0] == 1:
+            t = peer(offset)
+            relays.append(
+                remote(
+                    relay_out.at[pl.ds(pl.multiple_of(40 * (t - 8 * other_z), 8), 40)],
+                    state_in.at[me, pl.ds(pl.multiple_of(40 * other_z, 8), 40)],
+                    relay_send.at[k], relay_recv.at[k], (t, relay_blk),
+                )
+            )
+            relays[-1].start()
+
+    for copy in states + relays:
         copy.wait_recv()
 
     def solve(k, a, b):
@@ -318,13 +359,16 @@
         return alpha * a - beta * b, alpha * b + beta * a
 
     def source_of(v, carry):
-        for zh in range(2):
-            x = forward([state_in[n, v, zh] for n in range(NI)])
+        for half in range(2):
+            first = pl.multiple_of(v * 8 + half * 40, 8)
+            x = forward([state_in[n, pl.ds(first, 8), :] for n in range(NI)])
             for k in range(1, 8):
                 scale = table[2, k]
                 a, b = solve(k, -(scale * x[2 * k + 1]), scale * x[2 * k])
-                source[v, zh, 2 * k] = a
-                source[v, zh, 2 * k + 1] = b
+                for zh in range(2):
+                    rows = pl.ds(half * 4, 4)
+                    source[v, zh, 2 * k, rows, :] = a[zh * 4 : zh * 4 + 4]
+                    source[v, zh, 2 * k + 1, rows, :] = b[zh * 4 : zh * 4 + 4]
         return carry
 
     lax.fori_loop(0, 5, source_of, 0)
@@ -408,7 +452,7 @@
                 ]
                 x = backward(c)
                 for n in range(NI):
-                    change[n, v, zh] = x[n]
+                    change[n, v, :, pl.ds(128 * zh, 128)] = x[n]
             return carry
 
         lax.fori_loop(group[0], group[-1] + 1, smooth, 0)
@@ -419,16 +463,15 @@
             t = peer(offset)
             changes[g].append(
                 remote(
-                    change.at[t, vs], out.at[vs, :, here, :],
+                    change.at[t, vs], out.at[vs, here, :],
                     change_send.at[g, k], change_recv.at[g, k], (t, blk),
                 )
             )
             changes[g][-1].start()
         for v in group:
-            for zh in range(2):
-                out[v, zh, here, :] = change[me, v, zh]
-
-    for copies in [halos, states] + sweeps + rhs_copies:
+            out[v, here, :] = change[me, v]
+
+    for copies in [halos, states, relays] + sweeps + rhs_copies:
         for copy in copies:
             copy.wait_send()
     for copies in changes:
@@ -488,20 +531,23 @@
     peers = len(OFFSETS)
     groups = len(GROUPS)
     dma = pltpu.SemaphoreType.DMA
-    halves = state.reshape(5, 128, 2, 128).transpose(0, 2, 1, 3)
     change = pl.pallas_call(
         kernel,
-        out_shape=jax.ShapeDtypeStruct((5, 2, 128, 128), f32),
+        out_shape=jax.ShapeDtypeStruct((5, 128, 256), f32),
         in_specs=[
-            pl.BlockSpec(memory_space=pltpu.SMEM),
-            pl.BlockSpec(memory_space=pltpu.VMEM),
+            pl.BlockSpec(memory_space=pl.ANY),
+            pl.BlockSpec(memory_space=pl.ANY),
         ],
         out_specs=pl.BlockSpec(memory_space=pltpu.VMEM),
         scratch_shapes=[
+            pltpu.SMEM((7,), jnp.int32),
+            pltpu.VMEM((2, 5, 128, 128), f32),
             tiles(16), tiles(16), tiles(16),
             pltpu.VMEM((2, 5, 4, 8, 128), f32),
             tiles(16), tiles(16),
-            pltpu.VMEM((NI, 5, 2, 8, 128), f32),
+            pltpu.VMEM((NI * 80, 128), f32),
+            pltpu.VMEM((NI, 80, 128), f32),
+            pltpu.VMEM((8 * 40, 128), f32),
             pltpu.VMEM((NI * 80, 128), f32),
             pltpu.VMEM((NI, 80, 128), f32),
             pltpu.VMEM((3, 8, 8, 128), f32),
@@ -509,9 +555,11 @@
             pltpu.VMEM((5, 2, 14 * 16, 128), f32),
             pltpu.VMEM((2, 5, 2, 14 * 16, 128), f32),
             pltpu.VMEM((5, 2, 8 * 16, 128), f32),
-            pltpu.VMEM((NI, 5, 2, 8, 128), f32),
+            pltpu.VMEM((NI, 5, 8, 256), f32),
+            dma((3,)),
             dma((4,)), dma((4,)),
             dma((peers,)), dma((peers,)),
+            dma((8,)), dma((8,)),
             dma((groups, peers)), dma((groups, peers)),
             dma((groups, 2)), dma((groups, 2)),
             dma((groups, peers)), dma((groups, peers)),
@@ -519,8 +567,8 @@
         compiler_params=pltpu.CompilerParams(
             collective_id=0, has_side_effects=True, vmem_limit_bytes=40 * 2**20
         ),
-    )(multiples, halves)
-    return change.transpose(0, 2, 1, 3).reshape(state.shape)
+    )(multiples, state.reshape(5, 128, 256))
+    return change.reshape(state.shape)
 
 
 def solution(mesh):

time: 74.9 us -> 69.9 us (0.933)
  Pallas kernels: 70.8 us -> 67.1 us
  local copies, waits for them, and re-layouts: 3.98 us -> 2.58 us
    pallas_call x1, Pallas kernels: 70.8 us -> 67.1 us  [body(): pl.pallas_call(kernel, out_shape=jax.ShapeDtypeStruct((5, 128, 256), f32)...]
    reshape x3 -> x0, local copies, waits for them, and re-layouts: 2.82 us -> none  [the longest x2 1.46 us: body(): halves = state.reshape(5, 128, 2, 128).transpose(0, 2, 1, 3)]
    unnamed x2 -> x5, local copies, waits for them, and re-layouts: 0.65 us -> 2.58 us
where the time goes in v2:
time: 69.9 us; the launch traced here: 69.7 us
  Pallas kernels  67.1 us (96%)
  local copies, waits for them, and re-layouts  2.58 us (4%)
    pallas_call x1, Pallas kernels, body(): pl.pallas_call(kernel, out_shape=jax.ShapeDtypeStruct((5, 128, 256), f32)...  67.1 us
    unnamed x5, local copies, waits for them, and re-layouts  2.58 us

profile of v2, /device:TPU:1, one launch (start us, length us, event | category | flops | bytes accessed | tf_op | source)
XLA Modules:
  0.0 69.7 jit_solution(12804672030753280856)
XLA Ops:
  0.0 0.0 copy-start.1
  0.0 0.7 copy-done.1
  0.7 0.0 copy-start
  0.7 1.1 %copy-done = f32[1,5,16,8,256]{4,3,2,1,0:T(8,128)S(1)} copy-done((f32[1,5,16,8,256]{4,3,2,1,0:T(8,128)S(1)}, f32[1,5,16,8,256]{4,3,2,1,0:T(8,128)}, u32[]{:S(2)}) %copy-start) | copy-done | bytes 655384
  1.7 67.1 %shard_map.28 = f32[5,128,256]{2,1,0:T(8,128)S(1)} custom-call(s32[7]{0:T(128)S(1)} %copy-done.1, f32[5,128,256]{2,1,0:T(8,128)S(1)} %bitcast.3), custom_call_target="tpu_custom_call" | custom-call | tf_op jit(solution)/shard_map/pallas_call | solution.py:534
  68.9 0.8 %copy.4 = f32[1,5,16,8,256]{4,3,2,1,0:T(8,128)} copy(f32[1,5,16,8,256]{4,3,2,1,0:T(8,128)S(1)} %bitcast.2) | data formatting | bytes 1310720
Async XLA Ops:
  0.0 0.7 copy-start.1
  0.7 1.1 %copy-start = (f32[1,5,16,8,256]{4,3,2,1,0:T(8,128)S(1)}, f32[1,5,16,8,256]{4,3,2,1,0:T(8,128)}, u32[]{:S(2)}) copy-start(f32[1,5,16,8,256]{4,3,2,1,0:T(8,128)} %param.2) | copy-start | bytes 1966084

commit v3 on v2

--- a/solution.py
+++ b/solution.py
@@ -151,7 +151,7 @@
     multiples, state, cons, prim, acc, edges, prim2, acc2,
     state_out, state_in, relay_out, sweep_out, sweep_in, table, source,
     rhs, corr, last_corr, change,
-    load_sem, halo_send, halo_recv, state_send, state_recv, relay_send, relay_recv, sweep_send, sweep_recv,
+    told, load_sem, halo_send, halo_recv, state_send, state_recv, relay_send, relay_recv, sweep_send, sweep_recv,
     rhs_send, rhs_recv, change_send, change_recv,
 ):
     me = lax.axis_index("inst")
@@ -169,14 +169,20 @@
     other_z = 1 - my_z
 
     barrier = pltpu.get_barrier_semaphore()
+    partner = peer((0, 0, 1))
     for there in (up, down):
-        pl.semaphore_signal(barrier, inc=1, device_id=(me, there), device_id_type=MESH)
+        t = 8 * my_z + 2 * my_x + 1
+        pl.semaphore_signal(barrier, inc=1, device_id=(t, there), device_id_type=MESH)
     for offset in OFFSETS:
-        pl.semaphore_signal(barrier, inc=1, device_id=(peer(offset), blk), device_id_type=MESH)
-        if offset[0] == 1:
-            pl.semaphore_signal(
-                barrier, inc=1, device_id=(peer(offset), relay_blk), device_id_type=MESH
-            )
+        t = peer(offset)
+
+        @pl.when(lax.rem(t, 2) == 0)
+        def _():
+            pl.semaphore_signal(barrier, inc=1, device_id=(t, blk), device_id_type=MESH)
+
+    @pl.when(my_core == 0)
+    def _():
+        pl.semaphore_signal(barrier, inc=1, device_id=(partner, blk), device_id_type=MESH)
 
     loads = [
         pltpu.make_async_copy(
@@ -201,13 +207,46 @@
                 row = (c // 2) * 640 + (y // 4) * 40 + v * 8 + (c % 2) * 4 + y % 4
                 state_out[pl.ds(row, 8, stride=80), :] = s[v]
 
-    pl.semaphore_wait(barrier, NI - 1 + 2 + 8)
-
     def remote(source_ref, target_ref, send, recv, there):
         return pltpu.make_async_remote_copy(
             src_ref=source_ref, dst_ref=target_ref, send_sem=send, recv_sem=recv,
             device_id=there, device_id_type=MESH,
         )
+
+    states = []
+    for k, offset in enumerate(OFFSETS):
+        t = peer(offset)
+        first, rows = (0, 80) if offset[0] == 0 else (pl.multiple_of(40 * my_z, 8), 40)
+        states.append(
+            remote(
+                state_out.at[pl.ds(pl.multiple_of(80 * t + first, 8), rows)],
+                state_in.at[me, pl.ds(first, rows)],
+                state_send.at[k], state_recv.at[k], (t, blk),
+            )
+        )
+    own = state_out[pl.ds(pl.multiple_of(80 * me, 8), 80), :]
+    state_in[me] = own
+
+    def tell():
+        pl.semaphore_signal(told, inc=1, device_id=(partner, blk), device_id_type=MESH)
+
+    def send_states():
+        for copy in states:
+            copy.start()
+
+    @pl.when(my_core == 0)
+    def _():
+        pl.semaphore_wait(barrier, NI - 1)
+        tell()
+        send_states()
+        pl.semaphore_wait(told, 1)
+
+    @pl.when(my_core == 1)
+    def _():
+        pl.semaphore_wait(told, 1)
+        send_states()
+        pl.semaphore_wait(barrier, 5)
+        tell()
 
     halos = []
     for k, (mine, theirs, there) in enumerate(
@@ -274,21 +313,6 @@
 
     lax.fori_loop(0, 4, halo_axial_radial, 0)
     lax.fori_loop(4, 12, sweep2_axial_radial, 0)
-
-    states = []
-    for k, offset in enumerate(OFFSETS):
-        t = peer(offset)
-        first, rows = (0, 80) if offset[0] == 0 else (pl.multiple_of(40 * my_z, 8), 40)
-        states.append(
-            remote(
-                state_out.at[pl.ds(pl.multiple_of(80 * t + first, 8), rows)],
-                state_in.at[me, pl.ds(first, rows)],
-                state_send.at[k], state_recv.at[k], (t, blk),
-            )
-        )
-        states[-1].start()
-    own = state_out[pl.ds(pl.multiple_of(80 * me, 8), 80), :]
-    state_in[me] = own
 
     halos[2].wait_recv()
     halos[3].wait_recv()
@@ -556,6 +580,7 @@
             pltpu.VMEM((2, 5, 2, 14 * 16, 128), f32),
             pltpu.VMEM((5, 2, 8 * 16, 128), f32),
             pltpu.VMEM((NI, 5, 8, 256), f32),
+            pltpu.SemaphoreType.REGULAR,
             dma((3,)),
             dma((4,)), dma((4,)),
             dma((peers,)), dma((peers,)),

time: 69.9 us -> 66.8 us (0.956); the launches traced: 69.7 us -> 65.5 us
  Pallas kernels: 67.1 us -> 62.9 us
    pallas_call x1, Pallas kernels: 67.1 us -> 62.9 us  [body(): pl.pallas_call(kernel, out_shape=jax.ShapeDtypeStruct((5, 128, 256), f32)...]
where the time goes in v3:
time: 66.8 us; the launch traced here: 65.5 us
  Pallas kernels  62.9 us (94%)
  local copies, waits for them, and re-layouts  2.58 us (4%)
    pallas_call x1, Pallas kernels, body(): pl.pallas_call(kernel, out_shape=jax.ShapeDtypeStruct((5, 128, 256), f32)...  62.9 us
    unnamed x5, local copies, waits for them, and re-layouts  2.58 us

profile of v3, /device:TPU:1, one launch (start us, length us, event | category | flops | bytes accessed | tf_op | source)
XLA Modules:
  0.0 65.5 jit_solution(11432228350184131743)
XLA Ops:
  0.0 0.0 copy-start.1
  0.0 0.7 copy-done.1
  0.7 0.0 copy-start
  0.7 1.1 %copy-done = f32[1,5,16,8,256]{4,3,2,1,0:T(8,128)S(1)} copy-done((f32[1,5,16,8,256]{4,3,2,1,0:T(8,128)S(1)}, f32[1,5,16,8,256]{4,3,2,1,0:T(8,128)}, u32[]{:S(2)}) %copy-start) | copy-done | bytes 655384
  1.7 62.9 %shard_map.28 = f32[5,128,256]{2,1,0:T(8,128)S(1)} custom-call(s32[7]{0:T(128)S(1)} %copy-done.1, f32[5,128,256]{2,1,0:T(8,128)S(1)} %bitcast.3), custom_call_target="tpu_custom_call" | custom-call | tf_op jit(solution)/shard_map/pallas_call | solution.py:558
  64.7 0.8 %copy.4 = f32[1,5,16,8,256]{4,3,2,1,0:T(8,128)} copy(f32[1,5,16,8,256]{4,3,2,1,0:T(8,128)S(1)} %bitcast.2) | data formatting | bytes 1310720
Async XLA Ops:
  0.0 0.7 %copy-start.1 = (s32[7]{0:T(128)S(1)}, s32[7]{0:T(128)}, u32[]{:S(2)}) copy-start(s32[7]{0:T(128)} %multiples_hbm.1) | copy-start | bytes 88
  0.7 1.1 %copy-start = (f32[1,5,16,8,256]{4,3,2,1,0:T(8,128)S(1)}, f32[1,5,16,8,256]{4,3,2,1,0:T(8,128)}, u32[]{:S(2)}) copy-start(f32[1,5,16,8,256]{4,3,2,1,0:T(8,128)} %param.2) | copy-start | bytes 1966084
